TPU v7x, 32 devices: a whole 2x2x4 slice. The times are simulated.
32 devices in a mesh: sub: 4 (over y, core), grp: 8 (over z, x).
Axes of the slice: x: 2, y: 2, z: 4, core: 2. Of those that a mesh axis runs over, the one named last changes fastest.
Arguments:
- schur: bfloat16 [64, 1024, 1024], P(('sub', 'grp')), may hold values from -1 to 17, as said below
- local_inverse: bfloat16 [64, 1024, 1024], P(('sub', 'grp')), may hold values from -1 to 2, as said below
- coupling: float32 [64, 256], P(('sub', 'grp')), may hold values from 0.5 to 1.5
- basis: bfloat16 [64, 24, 1024], P(('sub', 'grp')), may hold values from -0.1875 to 0.1875
- coarse_map: int32 [64, 24], P(('sub', 'grp')), may hold values from 0 to 511
- coarse_count: int32 [64], P(('sub', 'grp')), may hold values from 12 to 24, as said below
- diag_inverse: float32 [16, 256, 256], P('grp'), may hold values from -1 to 1
- chain_factor: float32 [16, 256, 256], P('grp'), may hold values from -2 to 1
- residual: float32 [64, 1024, 384], P(('sub', 'grp')), may hold values from -18 to 18
- direction: float32 [64, 1024, 384], P(('sub', 'grp')), may hold values from -6 to 6
- rz_prev: float32 [384], replicated, may hold values from 32768 to 327680
Outputs:
- update: float32 [64, 1024, 384], P(('sub', 'grp'))
- residual_new: float32 [64, 1024, 384], P(('sub', 'grp'))
Inputs may be any that keep to these rules, and one draw needn't show every extreme that they name: `schur`: each block is symmetric positive definite. `local_inverse`: each block is symmetric positive definite. `coarse_count`: the first subdomain of each device has exactly 24 live slots.
All inputs are finite; a program needn't handle non-finite values.
Results may differ from a plain program's by a relative error of at most 0.0033.
Values sent between devices are 32-bit elements; how exact they have to be, the bound alone decides.
A program may use at most 64 MiB of HBM per device.

v0:
```python
import jax
import jax.numpy as jnp
from jax import lax
from jax.sharding import PartitionSpec as P


def shifted(value, axis, steps):
    count = lax.axis_size(axis)
    leading, last = (max(0, -steps), min(count, count - steps))
    return lax.ppermute(value, axis, [(source, source + steps) for source in range(leading, last)])


def product(left_side, right_side):
    return jnp.dot(
        left_side, right_side, precision=lax.Precision.HIGHEST, preferred_element_type=jnp.float32
    )


def forward_chain(sources, incoming, inverses, factors):

    def forward_advance(carried, pieces):
        inverse_block, factor_block, source_block = pieces
        fresh_value = product(inverse_block, source_block) - product(factor_block, carried)
        return (fresh_value, fresh_value)

    last_value, values = lax.scan(forward_advance, incoming, (inverses, factors, sources))
    return (values, last_value)


def backward_chain(values, incoming, inverses, factors):

    def backward_advance(carried, pieces):
        inverse_block, factor_block, value_block = pieces
        held_value = value_block - carried
        return (product(factor_block.T, held_value), product(inverse_block.T, held_value))

    outgoing, solved = lax.scan(
        backward_advance, incoming, (inverses, factors, values), reverse=True
    )
    return (outgoing, solved)


def assemble(values_in, targets, total_rows):
    selector = (jnp.arange(total_rows, dtype=jnp.int32)[:, None] == targets[None, :]).astype(
        jnp.float32
    )
    return product(selector, values_in)


def link_forward(values_in):
    return shifted(values_in, "grp", 1)


def link_backward(values_in):
    return shifted(values_in, "grp", -1)


def coarse_solve(sources, inverses, factors):
    super_count, block_size, col_count = sources.shape
    zero_in = jnp.zeros((block_size, col_count), jnp.float32)
    group_count = lax.axis_size("grp")
    unused_values, outgoing = forward_chain(sources, zero_in, inverses, factors)

    def forward_turn(turn_index, carried):
        return forward_chain(sources, link_forward(carried), inverses, factors)[1]

    outgoing = lax.fori_loop(0, group_count - 1, forward_turn, outgoing)
    values, unused_last = forward_chain(sources, link_forward(outgoing), inverses, factors)
    returned, unused_solved = backward_chain(values, zero_in, inverses, factors)

    def backward_turn(turn_index, carried):
        return backward_chain(values, link_backward(carried), inverses, factors)[0]

    returned = lax.fori_loop(0, group_count - 1, backward_turn, returned)
    unused_out, solved = backward_chain(values, link_backward(returned), inverses, factors)
    return solved


def shards(
    schur,
    local_inverse,
    coupling,
    basis,
    coarse_map,
    coarse_count,
    diag_inverse,
    chain_factor,
    residual,
    direction,
    rz_prev,
):
    local_subs, face_rows, col_count = residual.shape
    shared_rows = coupling.shape[1]
    slot_count = basis.shape[1]
    super_count = diag_inverse.shape[0]
    block_size = diag_inverse.shape[1]
    group_rows = super_count * block_size
    residual_low = residual.astype(jnp.bfloat16)
    local_part = jnp.einsum(
        "sfg,sgn->sfn", local_inverse, residual_low, preferred_element_type=jnp.float32
    )
    basis_wide = basis.astype(jnp.float32)
    coarse_local = jnp.einsum("scf,sfn->scn", basis_wide, residual, precision=lax.Precision.HIGHEST)
    slot_index = lax.broadcasted_iota(jnp.int32, (local_subs, slot_count), 1)
    live_slots = slot_index < coarse_count[:, None]
    coarse_local = jnp.where(live_slots[:, :, None], coarse_local, 0.0).reshape(
        local_subs * slot_count, col_count
    )
    targets = jnp.where(live_slots, coarse_map, -1).reshape(local_subs * slot_count)
    all_rows, all_targets = (
        lax.all_gather(coarse_local, "sub", axis=0, tiled=True),
        lax.all_gather(targets, "sub", axis=0, tiled=True),
    )
    sources = assemble(all_rows, all_targets, group_rows)
    source_cols = sources.shape[1]
    solved = coarse_solve(
        sources.reshape(super_count, block_size, source_cols), diag_inverse, chain_factor
    )
    solved = solved.reshape(group_rows, source_cols)
    picker = (targets[:, None] == jnp.arange(group_rows, dtype=jnp.int32)[None, :]).astype(
        jnp.float32
    )
    correction = product(picker, solved).reshape(local_subs, slot_count, col_count)
    precond = local_part + jnp.einsum(
        "scf,scn->sfn", basis_wide, correction, precision=lax.Precision.HIGHEST
    )
    precond_dot = lax.psum(jnp.sum(residual * precond, axis=(0, 1)), ("sub", "grp"))
    new_dir = precond + precond_dot / rz_prev * direction
    dir_low = new_dir.astype(jnp.bfloat16)
    applied = jnp.einsum("sfg,sgn->sfn", schur, dir_low, preferred_element_type=jnp.float32)
    from_before = shifted(new_dir[local_subs - 1, face_rows - shared_rows :], ("sub", "grp"), 1)
    prev_upper = jnp.concatenate(
        [from_before[None], new_dir[: local_subs - 1, face_rows - shared_rows :]], 0
    )
    lower_term = coupling[:, :, None] * prev_upper
    sent_back = coupling[:, :, None] * new_dir[:, :shared_rows]
    from_after = shifted(sent_back[0], ("sub", "grp"), -1)
    upper_term = jnp.concatenate([sent_back[1:], from_after[None]], 0)
    middle = jnp.zeros((local_subs, face_rows - 2 * shared_rows, col_count), jnp.float32)
    applied = applied - jnp.concatenate([lower_term, middle, upper_term], 1)
    curve_dot = lax.psum(jnp.sum(new_dir * applied, axis=(0, 1)), ("sub", "grp"))
    step_size = precond_dot / curve_dot
    return (step_size * new_dir, residual - step_size * applied)


def solution(mesh):
    return jax.shard_map(
        shards,
        mesh=mesh,
        in_specs=(
            P(("sub", "grp"), None, None),
            P(("sub", "grp"), None, None),
            P(("sub", "grp"), None),
            P(("sub", "grp"), None, None),
            P(("sub", "grp"), None),
            P(("sub", "grp")),
            P("grp", None, None),
            P("grp", None, None),
            P(("sub", "grp"), None, None),
            P(("sub", "grp"), None, None),
            P(),
        ),
        out_specs=(P(("sub", "grp"), None, None), P(("sub", "grp"), None, None)),
        check_vma=False,
    )
```

profile of v0, /device:TPU:0, one launch (start us, length us, event | category | flops | bytes accessed | tf_op | source)
XLA Modules:
  0.0 378.0 jit_solution(16870685378728506597)
XLA Ops:
  4.5 6.4 %all-reduce = s32[192]{0:T(256)S(1)} all-reduce(s32[192]{0:T(256)S(1)} %dynamic-update-slice), channel_id=1, replica_groups=mesh['sub'=4,'grp'=8] {'sub'}, use_global_device_ids=true, to_apply=%add | all-reduce | flops 192 | bytes 1536
  13.9 5.9 %all_gather.7 = f32[192,384]{1,0:T(8,128)S(1)} all-gather(f32[48,384]{1,0:T(8,128)S(1)} %bitcast.131), channel_id=1, replica_groups=mesh['sub'=4,'grp'=8] {'sub'}, dimensions={0}, use_global_device_ids=true | all-gather | bytes 368640 | tf_op jit(solution)/shard_map/all_gather | solution.py:111
  22.9 97.5 %while.109 = (s32[]{:T(128)}, f32[256,384]{1,0:T(8,128)S(1)}, f32[2,256,256]{2,1,0:T(8,128)S(1)}, f32[2,256,384]{2,1,0:T(8,128)S(1)}, f32[2,256,256]{2,1,0:T(8,128)S(1)}, /*index=5*/s32[]{:T(128)}, s32[]{:T(128)}, s32[]{:T(128)}) while((s32[]{:T(128)}, f32[256,384]{1,0:T(8,128)S(1)}, f32[2,256,256]{2,1,0:T(8,128)S(1)}, ...), condition=%wide.region_5.6_spmd, body=%wide.region_2.5_spmd.sunk | while | flops 604078080 | bytes 5637382 | solution.py:67
  26.4 8.8 %collective-permute-done.1 = f32[256,384]{1,0:T(8,128)S(1)} collective-permute-done((f32[256,384]{1,0:T(8,128)S(1)}, f32[256,384]{1,0:T(8,128)S(1)}, u32[]{:S(2)}, u32[]{:S(2)}) %collective-permute-start.1) | collective-permute-done | bytes 393248 | tf_op jit(solution)/shard_map/while/body/eval_jaxpr/ppermute | solution.py:10
  42.2 8.0 %collective-permute-done.1 = f32[256,384]{1,0:T(8,128)S(1)} collective-permute-done((f32[256,384]{1,0:T(8,128)S(1)}, f32[256,384]{1,0:T(8,128)S(1)}, u32[]{:S(2)}, u32[]{:S(2)}) %collective-permute-start.1) | collective-permute-done | bytes 393248 | tf_op jit(solution)/shard_map/while/body/eval_jaxpr/ppermute | solution.py:10
  57.2 7.1 %collective-permute-done.1 = f32[256,384]{1,0:T(8,128)S(1)} collective-permute-done((f32[256,384]{1,0:T(8,128)S(1)}, f32[256,384]{1,0:T(8,128)S(1)}, u32[]{:S(2)}, u32[]{:S(2)}) %collective-permute-start.1) | collective-permute-done | bytes 393248 | tf_op jit(solution)/shard_map/while/body/eval_jaxpr/ppermute | solution.py:10
  66.9 5.3 %collective-permute-start.1 = (f32[256,384]{1,0:T(8,128)S(1)}, f32[256,384]{1,0:T(8,128)S(1)}, u32[]{:S(2)}, u32[]{:S(2)}) collective-permute-start(f32[256,384]{1,0:T(8,128)S(1)} %get-tuple-element.954), channel_id=1, source_target_pairs={{0,1},{1,2},{2,3},{3,4},{4,5},{5,6},{6,7},{8,9},{9,10},{10,11},{11... | collective-permute-start | bytes 1179656 | tf_op jit(solution)/shard_map/while/body/eval_jaxpr/ppermute | solution.py:10
  72.2 6.2 %collective-permute-done.1 = f32[256,384]{1,0:T(8,128)S(1)} collective-permute-done((f32[256,384]{1,0:T(8,128)S(1)}, f32[256,384]{1,0:T(8,128)S(1)}, u32[]{:S(2)}, u32[]{:S(2)}) %collective-permute-start.1) | collective-permute-done | bytes 393248 | tf_op jit(solution)/shard_map/while/body/eval_jaxpr/ppermute | solution.py:10
  81.0 5.3 %collective-permute-start.1 = (f32[256,384]{1,0:T(8,128)S(1)}, f32[256,384]{1,0:T(8,128)S(1)}, u32[]{:S(2)}, u32[]{:S(2)}) collective-permute-start(f32[256,384]{1,0:T(8,128)S(1)} %get-tuple-element.954), channel_id=1, source_target_pairs={{0,1},{1,2},{2,3},{3,4},{4,5},{5,6},{6,7},{8,9},{9,10},{10,11},{11... | collective-permute-start | bytes 1179656 | tf_op jit(solution)/shard_map/while/body/eval_jaxpr/ppermute | solution.py:10
  86.3 5.3 %collective-permute-done.1 = f32[256,384]{1,0:T(8,128)S(1)} collective-permute-done((f32[256,384]{1,0:T(8,128)S(1)}, f32[256,384]{1,0:T(8,128)S(1)}, u32[]{:S(2)}, u32[]{:S(2)}) %collective-permute-start.1) | collective-permute-done | bytes 393248 | tf_op jit(solution)/shard_map/while/body/eval_jaxpr/ppermute | solution.py:10
  94.2 5.3 %collective-permute-start.1 = (f32[256,384]{1,0:T(8,128)S(1)}, f32[256,384]{1,0:T(8,128)S(1)}, u32[]{:S(2)}, u32[]{:S(2)}) collective-permute-start(f32[256,384]{1,0:T(8,128)S(1)} %get-tuple-element.954), channel_id=1, source_target_pairs={{0,1},{1,2},{2,3},{3,4},{4,5},{5,6},{6,7},{8,9},{9,10},{10,11},{11... | collective-permute-start | bytes 1179656 | tf_op jit(solution)/shard_map/while/body/eval_jaxpr/ppermute | solution.py:10
  99.5 5.3 %collective-permute-done.1 = f32[256,384]{1,0:T(8,128)S(1)} collective-permute-done((f32[256,384]{1,0:T(8,128)S(1)}, f32[256,384]{1,0:T(8,128)S(1)}, u32[]{:S(2)}, u32[]{:S(2)}) %collective-permute-start.1) | collective-permute-done | bytes 393248 | tf_op jit(solution)/shard_map/while/body/eval_jaxpr/ppermute | solution.py:10
  107.3 5.3 %collective-permute-start.1 = (f32[256,384]{1,0:T(8,128)S(1)}, f32[256,384]{1,0:T(8,128)S(1)}, u32[]{:S(2)}, u32[]{:S(2)}) collective-permute-start(f32[256,384]{1,0:T(8,128)S(1)} %get-tuple-element.954), channel_id=1, source_target_pairs={{0,1},{1,2},{2,3},{3,4},{4,5},{5,6},{6,7},{8,9},{9,10},{10,11},{11... | collective-permute-start | bytes 1179656 | tf_op jit(solution)/shard_map/while/body/eval_jaxpr/ppermute | solution.py:10
  112.6 5.3 %collective-permute-done.1 = f32[256,384]{1,0:T(8,128)S(1)} collective-permute-done((f32[256,384]{1,0:T(8,128)S(1)}, f32[256,384]{1,0:T(8,128)S(1)}, u32[]{:S(2)}, u32[]{:S(2)}) %collective-permute-start.1) | collective-permute-done | bytes 393248 | tf_op jit(solution)/shard_map/while/body/eval_jaxpr/ppermute | solution.py:10
  120.4 5.3 %collective-permute-start.2 = (f32[256,384]{1,0:T(8,128)S(1)}, f32[256,384]{1,0:T(8,128)S(1)}, u32[]{:S(2)}, u32[]{:S(2)}) collective-permute-start(f32[256,384]{1,0:T(8,128)S(1)} %get-tuple-element.506), channel_id=1, source_target_pairs={{0,1},{1,2},{2,3},{3,4},{4,5},{5,6},{6,7},{8,9},{9,10},{10,11},{11... | collective-permute-start | bytes 1179656 | tf_op jit(solution)/shard_map/ppermute | solution.py:10
  125.8 5.3 %collective-permute-done.2 = f32[256,384]{1,0:T(8,128)S(1)} collective-permute-done((f32[256,384]{1,0:T(8,128)S(1)}, f32[256,384]{1,0:T(8,128)S(1)}, u32[]{:S(2)}, u32[]{:S(2)}) %collective-permute-start.2) | collective-permute-done | bytes 393248 | tf_op jit(solution)/shard_map/ppermute | solution.py:10
  135.1 101.7 %while.113 = (s32[]{:T(128)}, f32[256,384]{1,0:T(8,128)S(1)}, f32[2,256,256]{2,1,0:T(8,128)S(1)}, f32[2,256,384]{2,1,0:T(8,128)S(1)}, s32[]{:T(128)}, /*index=5*/s32[]{:T(128)}, s32[]{:T(128)}) while((s32[]{:T(128)}, f32[256,384]{1,0:T(8,128)S(1)}, f32[2,256,256]{2,1,0:T(8,128)S(1)}, f32[2,256,384]{2,1,0:T(8,128)S(1)}, s32[]{:T(128)}, ...), condition=%wide.region_13.14_spmd, body=%wide.region_10.13_spmd.sunk | while | flops 302088192 | bytes 4588782 | solution.py:74
  136.4 10.8 %collective-permute-done = f32[256,384]{1,0:T(8,128)S(1)} collective-permute-done((f32[256,384]{1,0:T(8,128)S(1)}, f32[256,384]{1,0:T(8,128)S(1)}, u32[]{:S(2)}, u32[]{:S(2)}) %collective-permute-start) | collective-permute-done | bytes 393248 | tf_op jit(solution)/shard_map/while/body/eval_jaxpr/ppermute | solution.py:10
  149.9 13.1 %collective-permute-done = f32[256,384]{1,0:T(8,128)S(1)} collective-permute-done((f32[256,384]{1,0:T(8,128)S(1)}, f32[256,384]{1,0:T(8,128)S(1)}, u32[]{:S(2)}, u32[]{:S(2)}) %collective-permute-start) | collective-permute-done | bytes 393248 | tf_op jit(solution)/shard_map/while/body/eval_jaxpr/ppermute | solution.py:10
  165.8 14.5 %collective-permute-done = f32[256,384]{1,0:T(8,128)S(1)} collective-permute-done((f32[256,384]{1,0:T(8,128)S(1)}, f32[256,384]{1,0:T(8,128)S(1)}, u32[]{:S(2)}, u32[]{:S(2)}) %collective-permute-start) | collective-permute-done | bytes 393248 | tf_op jit(solution)/shard_map/while/body/eval_jaxpr/ppermute | solution.py:10
  183.0 12.4 %collective-permute-done = f32[256,384]{1,0:T(8,128)S(1)} collective-permute-done((f32[256,384]{1,0:T(8,128)S(1)}, f32[256,384]{1,0:T(8,128)S(1)}, u32[]{:S(2)}, u32[]{:S(2)}) %collective-permute-start) | collective-permute-done | bytes 393248 | tf_op jit(solution)/shard_map/while/body/eval_jaxpr/ppermute | solution.py:10
  198.1 11.5 %collective-permute-done = f32[256,384]{1,0:T(8,128)S(1)} collective-permute-done((f32[256,384]{1,0:T(8,128)S(1)}, f32[256,384]{1,0:T(8,128)S(1)}, u32[]{:S(2)}, u32[]{:S(2)}) %collective-permute-start) | collective-permute-done | bytes 393248 | tf_op jit(solution)/shard_map/while/body/eval_jaxpr/ppermute | solution.py:10
  212.3 10.6 %collective-permute-done = f32[256,384]{1,0:T(8,128)S(1)} collective-permute-done((f32[256,384]{1,0:T(8,128)S(1)}, f32[256,384]{1,0:T(8,128)S(1)}, u32[]{:S(2)}, u32[]{:S(2)}) %collective-permute-start) | collective-permute-done | bytes 393248 | tf_op jit(solution)/shard_map/while/body/eval_jaxpr/ppermute | solution.py:10
  225.6 9.6 %collective-permute-done = f32[256,384]{1,0:T(8,128)S(1)} collective-permute-done((f32[256,384]{1,0:T(8,128)S(1)}, f32[256,384]{1,0:T(8,128)S(1)}, u32[]{:S(2)}, u32[]{:S(2)}) %collective-permute-start) | collective-permute-done | bytes 393248 | tf_op jit(solution)/shard_map/while/body/eval_jaxpr/ppermute | solution.py:10
  238.2 7.2 %fusion.50 = f32[2,1024,384]{2,1,0:T(8,128)} fusion(bf16[2,1024,1024]{2,1,0:T(8,128)(2,1)} %param.28, f32[2,1024,384]{2,1,0:T(8,128)} %param.35), kind=kOutput, calls=%fused_computation.65 | convolution fusion | flops 1611399168 | bytes 10485760 | tf_op jit(solution)/shard_map/sfg,sgn->sfn/dot_general | solution.py:99
  250.2 6.2 %multiply_reduce_fusion.1 = (f32[384]{0:T(512)S(1)}, f32[2,1024,384]{2,1,0:T(8,128)}) fusion(f32[2,1024,384]{2,1,0:T(8,128)} %param.35, f32[2,1024,384]{2,1,0:T(8,128)} %fusion.50, f32[2,24,384]{2,1,0:T(8,128)S(1)} %fusion.55, bf16[2,24,1024]{2,1,0:T(8,128)(2,1)S(1)} %copy-done), kind=kOutput, calls=%fused_computation.62 | convolution fusion | flops 228851328 | bytes 9610752 | tf_op jit(solution)/shard_map/scf,scn->sfn/dot_general | solution.py:124
  256.4 41.1 %psum.14 = f32[384]{0:T(512)S(1)} all-reduce(f32[384]{0:T(512)S(1)} %get-tuple-element.617), channel_id=1, replica_groups=mesh['sub'=4,'grp'=8] {'sub','grp'}, use_global_device_ids=true, to_apply=%region_17.18 | all-reduce | flops 384 | bytes 3072 | tf_op jit(solution)/shard_map/psum | solution.py:127
  300.8 4.5 %collective-permute-start.4 = (f32[256,384]{1,0:T(8,128)S(1)}, f32[256,384]{1,0:T(8,128)S(1)}, u32[]{:S(2)}, u32[]{:S(2)}) collective-permute-start(f32[256,384]{1,0:T(8,128)S(1)} %get-tuple-element.609), channel_id=1, source_target_pairs={{0,1},{1,2},{2,3},{3,4},{4,5},{5,6},{6,7},{7,8},{8,9},{9,10},{10,1... | collective-permute-start | bytes 1179656 | tf_op jit(solution)/shard_map/ppermute | solution.py:10
  305.2 7.3 %collective-permute-done.4 = f32[256,384]{1,0:T(8,128)S(1)} collective-permute-done((f32[256,384]{1,0:T(8,128)S(1)}, f32[256,384]{1,0:T(8,128)S(1)}, u32[]{:S(2)}, u32[]{:S(2)}) %collective-permute-start.4) | collective-permute-done | bytes 393248 | tf_op jit(solution)/shard_map/ppermute | solution.py:10
  314.1 11.9 %collective-permute-done.5 = f32[256,384]{1,0:T(8,128)S(1)} collective-permute-done((f32[256,384]{1,0:T(8,128)S(1)}, f32[256,384]{1,0:T(8,128)S(1)}, u32[]{:S(2)}, u32[]{:S(2)}) %collective-permute-start.5) | collective-permute-done | bytes 393248 | tf_op jit(solution)/shard_map/ppermute | solution.py:10
  330.0 41.0 %psum.15 = f32[384]{0:T(512)S(1)} all-reduce(f32[384]{0:T(512)S(1)} %get-tuple-element.619), channel_id=1, replica_groups=mesh['sub'=4,'grp'=8] {'sub','grp'}, use_global_device_ids=true, to_apply=%region_19.20 | all-reduce | flops 384 | bytes 3072 | tf_op jit(solution)/shard_map/psum | solution.py:141
  371.0 7.0 %multiply_subtract_fusion = (f32[2,1024,384]{2,1,0:T(8,128)}, f32[2,1024,384]{2,1,0:T(8,128)}) fusion(f32[2,1024,384]{2,1,0:T(8,128)} %param.35, f32[2,1024,384]{2,1,0:T(8,128)} %get-tuple-element.620, f32[384]{0:T(512)S(1)} %div.7, f32[2,1024,384]{2,1,0:T(8,128)} %copy-done.3), kind=kLoop, calls=%fused_computation.59 | loop fusion | flops 2359296 | bytes 15730176 | tf_op jit(solution)/shard_map/sub | solution.py:143
  (173 shorter events, 112.6 us)
Async XLA Ops:
  0.6 10.2 %copy-start = (bf16[2,24,1024]{2,1,0:T(8,128)(2,1)S(1)}, bf16[2,24,1024]{2,1,0:T(8,128)(2,1)}, u32[]{:S(2)}) copy-start(bf16[2,24,1024]{2,1,0:T(8,128)(2,1)} %param.30) | copy-start | bytes 294916
  0.6 19.7 %copy-start.1 = (f32[2,256,256]{2,1,0:T(8,128)S(1)}, f32[2,256,256]{2,1,0:T(8,128)}, u32[]{:S(2)}) copy-start(f32[2,256,256]{2,1,0:T(8,128)} %param.34) | copy-start | bytes 1572868
  0.7 19.7 %copy-start.2 = (f32[2,256,256]{2,1,0:T(8,128)S(1)}, f32[2,256,256]{2,1,0:T(8,128)}, u32[]{:S(2)}) copy-start(f32[2,256,256]{2,1,0:T(8,128)} %param.33) | copy-start | bytes 1572868
  23.0 12.3 %collective-permute-start.1 = (f32[256,384]{1,0:T(8,128)S(1)}, f32[256,384]{1,0:T(8,128)S(1)}, u32[]{:S(2)}, u32[]{:S(2)}) collective-permute-start(f32[256,384]{1,0:T(8,128)S(1)} %get-tuple-element.954), channel_id=1, source_target_pairs={{0,1},{1,2},{2,3},{3,4},{4,5},{5,6},{6,7},{8,9},{9,10},{10,11},{11... | collective-permute-start | bytes 1179656 | tf_op jit(solution)/shard_map/while/body/eval_jaxpr/ppermute | solution.py:10
  37.8 12.4 %collective-permute-start.1 = (f32[256,384]{1,0:T(8,128)S(1)}, f32[256,384]{1,0:T(8,128)S(1)}, u32[]{:S(2)}, u32[]{:S(2)}) collective-permute-start(f32[256,384]{1,0:T(8,128)S(1)} %get-tuple-element.954), channel_id=1, source_target_pairs={{0,1},{1,2},{2,3},{3,4},{4,5},{5,6},{6,7},{8,9},{9,10},{10,11},{11... | collective-permute-start | bytes 1179656 | tf_op jit(solution)/shard_map/while/body/eval_jaxpr/ppermute | solution.py:10
  52.8 11.5 %collective-permute-start.1 = (f32[256,384]{1,0:T(8,128)S(1)}, f32[256,384]{1,0:T(8,128)S(1)}, u32[]{:S(2)}, u32[]{:S(2)}) collective-permute-start(f32[256,384]{1,0:T(8,128)S(1)} %get-tuple-element.954), channel_id=1, source_target_pairs={{0,1},{1,2},{2,3},{3,4},{4,5},{5,6},{6,7},{8,9},{9,10},{10,11},{11... | collective-permute-start | bytes 1179656 | tf_op jit(solution)/shard_map/while/body/eval_jaxpr/ppermute | solution.py:10
  66.9 11.5 %collective-permute-start.1 = (f32[256,384]{1,0:T(8,128)S(1)}, f32[256,384]{1,0:T(8,128)S(1)}, u32[]{:S(2)}, u32[]{:S(2)}) collective-permute-start(f32[256,384]{1,0:T(8,128)S(1)} %get-tuple-element.954), channel_id=1, source_target_pairs={{0,1},{1,2},{2,3},{3,4},{4,5},{5,6},{6,7},{8,9},{9,10},{10,11},{11... | collective-permute-start | bytes 1179656 | tf_op jit(solution)/shard_map/while/body/eval_jaxpr/ppermute | solution.py:10
  81.0 10.6 %collective-permute-start.1 = (f32[256,384]{1,0:T(8,128)S(1)}, f32[256,384]{1,0:T(8,128)S(1)}, u32[]{:S(2)}, u32[]{:S(2)}) collective-permute-start(f32[256,384]{1,0:T(8,128)S(1)} %get-tuple-element.954), channel_id=1, source_target_pairs={{0,1},{1,2},{2,3},{3,4},{4,5},{5,6},{6,7},{8,9},{9,10},{10,11},{11... | collective-permute-start | bytes 1179656 | tf_op jit(solution)/shard_map/while/body/eval_jaxpr/ppermute | solution.py:10
  94.2 10.6 %collective-permute-start.1 = (f32[256,384]{1,0:T(8,128)S(1)}, f32[256,384]{1,0:T(8,128)S(1)}, u32[]{:S(2)}, u32[]{:S(2)}) collective-permute-start(f32[256,384]{1,0:T(8,128)S(1)} %get-tuple-element.954), channel_id=1, source_target_pairs={{0,1},{1,2},{2,3},{3,4},{4,5},{5,6},{6,7},{8,9},{9,10},{10,11},{11... | collective-permute-start | bytes 1179656 | tf_op jit(solution)/shard_map/while/body/eval_jaxpr/ppermute | solution.py:10
  107.3 10.6 %collective-permute-start.1 = (f32[256,384]{1,0:T(8,128)S(1)}, f32[256,384]{1,0:T(8,128)S(1)}, u32[]{:S(2)}, u32[]{:S(2)}) collective-permute-start(f32[256,384]{1,0:T(8,128)S(1)} %get-tuple-element.954), channel_id=1, source_target_pairs={{0,1},{1,2},{2,3},{3,4},{4,5},{5,6},{6,7},{8,9},{9,10},{10,11},{11... | collective-permute-start | bytes 1179656 | tf_op jit(solution)/shard_map/while/body/eval_jaxpr/ppermute | solution.py:10
  120.4 10.6 %collective-permute-start.2 = (f32[256,384]{1,0:T(8,128)S(1)}, f32[256,384]{1,0:T(8,128)S(1)}, u32[]{:S(2)}, u32[]{:S(2)}) collective-permute-start(f32[256,384]{1,0:T(8,128)S(1)} %get-tuple-element.506), channel_id=1, source_target_pairs={{0,1},{1,2},{2,3},{3,4},{4,5},{5,6},{6,7},{8,9},{9,10},{10,11},{11... | collective-permute-start | bytes 1179656 | tf_op jit(solution)/shard_map/ppermute | solution.py:10
  135.1 12.1 %collective-permute-start = (f32[256,384]{1,0:T(8,128)S(1)}, f32[256,384]{1,0:T(8,128)S(1)}, u32[]{:S(2)}, u32[]{:S(2)}) collective-permute-start(f32[256,384]{1,0:T(8,128)S(1)} %get-tuple-element.1013), channel_id=1, source_target_pairs={{1,0},{2,1},{3,2},{4,3},{5,4},{6,5},{7,6},{9,8},{10,9},{11,10},{12... | collective-permute-start | bytes 1179656 | tf_op jit(solution)/shard_map/while/body/eval_jaxpr/ppermute | solution.py:10
  148.6 14.4 %collective-permute-start = (f32[256,384]{1,0:T(8,128)S(1)}, f32[256,384]{1,0:T(8,128)S(1)}, u32[]{:S(2)}, u32[]{:S(2)}) collective-permute-start(f32[256,384]{1,0:T(8,128)S(1)} %get-tuple-element.1013), channel_id=1, source_target_pairs={{1,0},{2,1},{3,2},{4,3},{5,4},{6,5},{7,6},{9,8},{10,9},{11,10},{12... | collective-permute-start | bytes 1179656 | tf_op jit(solution)/shard_map/while/body/eval_jaxpr/ppermute | solution.py:10
  164.5 15.8 %collective-permute-start = (f32[256,384]{1,0:T(8,128)S(1)}, f32[256,384]{1,0:T(8,128)S(1)}, u32[]{:S(2)}, u32[]{:S(2)}) collective-permute-start(f32[256,384]{1,0:T(8,128)S(1)} %get-tuple-element.1013), channel_id=1, source_target_pairs={{1,0},{2,1},{3,2},{4,3},{5,4},{6,5},{7,6},{9,8},{10,9},{11,10},{12... | collective-permute-start | bytes 1179656 | tf_op jit(solution)/shard_map/while/body/eval_jaxpr/ppermute | solution.py:10
  181.7 13.7 %collective-permute-start = (f32[256,384]{1,0:T(8,128)S(1)}, f32[256,384]{1,0:T(8,128)S(1)}, u32[]{:S(2)}, u32[]{:S(2)}) collective-permute-start(f32[256,384]{1,0:T(8,128)S(1)} %get-tuple-element.1013), channel_id=1, source_target_pairs={{1,0},{2,1},{3,2},{4,3},{5,4},{6,5},{7,6},{9,8},{10,9},{11,10},{12... | collective-permute-start | bytes 1179656 | tf_op jit(solution)/shard_map/while/body/eval_jaxpr/ppermute | solution.py:10
  196.8 12.8 %collective-permute-start = (f32[256,384]{1,0:T(8,128)S(1)}, f32[256,384]{1,0:T(8,128)S(1)}, u32[]{:S(2)}, u32[]{:S(2)}) collective-permute-start(f32[256,384]{1,0:T(8,128)S(1)} %get-tuple-element.1013), channel_id=1, source_target_pairs={{1,0},{2,1},{3,2},{4,3},{5,4},{6,5},{7,6},{9,8},{10,9},{11,10},{12... | collective-permute-start | bytes 1179656 | tf_op jit(solution)/shard_map/while/body/eval_jaxpr/ppermute | solution.py:10
  211.0 11.9 %collective-permute-start = (f32[256,384]{1,0:T(8,128)S(1)}, f32[256,384]{1,0:T(8,128)S(1)}, u32[]{:S(2)}, u32[]{:S(2)}) collective-permute-start(f32[256,384]{1,0:T(8,128)S(1)} %get-tuple-element.1013), channel_id=1, source_target_pairs={{1,0},{2,1},{3,2},{4,3},{5,4},{6,5},{7,6},{9,8},{10,9},{11,10},{12... | collective-permute-start | bytes 1179656 | tf_op jit(solution)/shard_map/while/body/eval_jaxpr/ppermute | solution.py:10
  224.3 10.9 %collective-permute-start = (f32[256,384]{1,0:T(8,128)S(1)}, f32[256,384]{1,0:T(8,128)S(1)}, u32[]{:S(2)}, u32[]{:S(2)}) collective-permute-start(f32[256,384]{1,0:T(8,128)S(1)} %get-tuple-element.1013), channel_id=1, source_target_pairs={{1,0},{2,1},{3,2},{4,3},{5,4},{6,5},{7,6},{9,8},{10,9},{11,10},{12... | collective-permute-start | bytes 1179656 | tf_op jit(solution)/shard_map/while/body/eval_jaxpr/ppermute | solution.py:10
  236.7 10.3 %collective-permute-start.3 = (f32[256,384]{1,0:T(8,128)S(1)}, f32[256,384]{1,0:T(8,128)S(1)}, u32[]{:S(2)}, u32[]{:S(2)}) collective-permute-start(f32[256,384]{1,0:T(8,128)S(1)} %get-tuple-element.509), channel_id=1, source_target_pairs={{1,0},{2,1},{3,2},{4,3},{5,4},{6,5},{7,6},{9,8},{10,9},{11,10},{12... | collective-permute-start | bytes 1179656 | tf_op jit(solution)/shard_map/ppermute | solution.py:10
  250.2 47.3 %copy-start.4 = (f32[384]{0:T(512)S(1)}, f32[384]{0:T(512)}, u32[]{:S(2)}) copy-start(f32[384]{0:T(512)} %param.37) | copy-start | bytes 4612
  297.5 15.0 %copy-start.5 = (f32[2,256]{1,0:T(2,128)S(1)}, f32[2,256]{1,0:T(2,128)}, u32[]{:S(2)}) copy-start(f32[2,256]{1,0:T(2,128)} %param.29) | copy-start | bytes 6148
  300.7 25.3 %copy-start.3 = (f32[2,1024,384]{2,1,0:T(8,128)}, f32[2,1024,384]{2,1,0:T(8,128)S(1)}, u32[]{:S(2)}) copy-start(f32[2,1024,384]{2,1,0:T(8,128)S(1)} %multiply_add_fusion) | copy-start | bytes 9437188
  300.7 25.3 %copy-start.6 = (bf16[2,1024,1024]{2,1,0:T(8,128)(2,1)S(1)}, bf16[2,1024,1024]{2,1,0:T(8,128)(2,1)}, u32[]{:S(2)}) copy-start(bf16[2,1024,1024]{2,1,0:T(8,128)(2,1)} %param.27) | copy-start | bytes 12582916
  300.8 11.7 %collective-permute-start.4 = (f32[256,384]{1,0:T(8,128)S(1)}, f32[256,384]{1,0:T(8,128)S(1)}, u32[]{:S(2)}, u32[]{:S(2)}) collective-permute-start(f32[256,384]{1,0:T(8,128)S(1)} %get-tuple-element.609), channel_id=1, source_target_pairs={{0,1},{1,2},{2,3},{3,4},{4,5},{5,6},{6,7},{7,8},{8,9},{9,10},{10,1... | collective-permute-start | bytes 1179656 | tf_op jit(solution)/shard_map/ppermute | solution.py:10
  312.7 13.2 %collective-permute-start.5 = (f32[256,384]{1,0:T(8,128)S(1)}, f32[256,384]{1,0:T(8,128)S(1)}, u32[]{:S(2)}, u32[]{:S(2)}) collective-permute-start(f32[256,384]{1,0:T(8,128)S(1)} %get-tuple-element.612), channel_id=1, source_target_pairs={{1,0},{2,1},{3,2},{4,3},{5,4},{6,5},{7,6},{8,7},{9,8},{10,9},{11,1... | collective-permute-start | bytes 1179656 | tf_op jit(solution)/shard_map/ppermute | solution.py:10
where the time goes:
time: 379 us; the launch traced here: 378 us
  waiting for transfers between devices  155 us (41%)
  blocking collectives  94.3 us (25%)
  matrix products  55.7 us (15%)
  starting transfers between devices  55 us (15%)
  other arithmetic  11.9 us (3%)
    ppermute x18, waiting for transfers between devices, shifted(): lax.ppermute(value, axis, [(source, source + steps) for source in range(l...  155 us
    ppermute x18, starting transfers between devices, shifted(): lax.ppermute(value, axis, [(source, source + steps) for source in range(l...  55 us
    psum x1, blocking collectives, shards(): lax.psum(jnp.sum(residual * precond, axis=(0, 1)), ('sub', 'grp'))  41.1 us
    psum x1, blocking collectives, shards(): lax.psum(jnp.sum(new_dir * applied, axis=(0, 1)), ('sub', 'grp'))  41 us
    dot_general x58, matrix products, product(): jnp.dot(left_side, right_side, precision=lax.Precision.HIGHEST, preferred...  35.4 us
  transfers between devices with their start and end apart: 18, of which 18 were waited for; matrix products, arithmetic and copies ran while one was open for 2% of the time, Pallas kernels for 0%

commit v1 on v0

v1 whole, which is shorter than its diff:
```python
import functools

import jax
import jax.numpy as jnp
from jax import lax
from jax.experimental import pallas as pl
from jax.experimental.pallas import tpu as pltpu
from jax.sharding import PartitionSpec as P

F32 = jnp.float32
BF16 = jnp.bfloat16
NN = (((1,), (0,)), ((), ()))
NT = (((1,), (1,)), ((), ()))
LANE = 128
CHUNK = 256


def mm(a, b, dims=NN):
    return lax.dot_general(a, b, dims, preferred_element_type=F32)


def split(x):
    hi = x.astype(BF16)
    return hi, (x - hi.astype(F32)).astype(BF16)


def mm3(a, b, dims=NN):
    return mm(a[0], b[0], dims) + (mm(a[0], b[1], dims) + mm(a[1], b[0], dims))


def kernel(
    n_sub,
    n_grp,
    count_ref,
    coup_ref,
    basis_ref,
    cmap_ref,
    rzp_ref,
    schur_h,
    linv_h,
    diag_h,
    chain_h,
    res_h,
    dir_h,
    upd_h,
    new_h,
    sv,
    iv,
    dv,
    lv,
    rv,
    pv,
    rhi,
    xhi,
    xlo,
    lp,
    ulp,
    ud,
    bt,
    wcat,
    btedge,
    kown,
    knext,
    mapv,
    tsend,
    trecv,
    rsend,
    rrecv,
    asend,
    arecv,
    amat,
    lmat,
    fmat,
    e0v,
    bv,
    brecv,
    bpl,
    yin,
    yout,
    y0v,
    y1v,
    qsend,
    qrecv,
    tin,
    tout,
    csend,
    crecv,
    cbuf,
    chalo,
    dhalo,
    lhalo,
    bhalo,
    clv,
    gmat,
    mmat,
    sums,
    gath1,
    mid,
    gath2,
    load_sem,
    out_sem,
    t_sem,
    r_sem,
    a_sem,
    b_sem,
    y_sem,
    q_sem,
    ti_sem,
    c_sem,
    ch_sem,
    dh_sem,
    lh_sem,
    bh_sem,
    kn_sem,
    s1_sem,
    s2_sem,
):
    s = lax.axis_index("sub")
    g = lax.axis_index("grp")
    odd = lax.rem(g, 2) == 1
    even = jnp.logical_not(odd)
    plane = g // 2
    n_plane = n_grp // 2
    first_plane = plane == 0
    last_plane = plane == n_plane - 1
    faces, cols = rv.shape[1], rv.shape[2]
    share = coup_ref.shape[1]
    slots = basis_ref.shape[1]
    blk = dv.shape[1]
    part = cols // n_sub
    wide = n_sub * LANE
    me = s * n_grp + g
    has_prev = me > 0
    has_next = me < n_sub * n_grp - 1
    prev_at = {"sub": jnp.where(g > 0, s, s - 1), "grp": jnp.where(g > 0, g - 1, n_grp - 1)}
    next_at = {
        "sub": jnp.where(g < n_grp - 1, s, s + 1),
        "grp": jnp.where(g < n_grp - 1, g + 1, 0),
    }
    pair_at = {"grp": jnp.where(odd, g - 1, g + 1)}

    def remote(src, dst, sems, k, where):
        return pltpu.make_async_remote_copy(
            src_ref=src,
            dst_ref=dst,
            send_sem=sems.at[0, k],
            recv_sem=sems.at[1, k],
            device_id=where,
            device_id_type=pl.DeviceIdType.MESH,
        )

    def load(src, dst, k):
        return pltpu.make_async_copy(src, dst, load_sem.at[k])

    ld_r = [load(res_h.at[j], rv.at[j], j) for j in range(2)]
    ld_l = load(chain_h, lv, 2)
    ld_d = load(diag_h, dv, 3)
    ld_i = load(linv_h, iv, 4)
    ld_p = load(dir_h, pv, 5)
    ld_s = load(schur_h, sv, 6)
    for c in ld_r + [ld_l, ld_d, ld_i, ld_p, ld_s]:
        c.start()

    barrier = pltpu.get_barrier_semaphore()
    for k in range(1, n_sub):
        pl.semaphore_signal(
            barrier, inc=1, device_id={"sub": lax.rem(s + k, n_sub)},
            device_id_type=pl.DeviceIdType.MESH,
        )
    for k in range(1, n_grp):
        pl.semaphore_signal(
            barrier, inc=1, device_id={"grp": lax.rem(g + k, n_grp)},
            device_id_type=pl.DeviceIdType.MESH,
        )
    wrap_prev = jnp.logical_and(g == 0, s > 0)
    wrap_next = jnp.logical_and(g == n_grp - 1, s < n_sub - 1)

    @pl.when(wrap_prev)
    def _():
        pl.semaphore_signal(
            barrier, inc=1, device_id=prev_at, device_id_type=pl.DeviceIdType.MESH
        )

    @pl.when(wrap_next)
    def _():
        pl.semaphore_signal(
            barrier, inc=1, device_id=next_at, device_id_type=pl.DeviceIdType.MESH
        )

    mapv[...] = jnp.zeros_like(mapv)
    mapv[0:2, 0:slots] = cmap_ref[...]
    lane = lax.broadcasted_iota(jnp.int32, (1, LANE), 1)
    one = jnp.where(lane < count_ref[0], mapv[0:1, :], -1).astype(F32)
    two = jnp.where(lane < count_ref[1], mapv[1:2, :], -1).astype(F32)
    two = pltpu.roll(jnp.broadcast_to(two, (8, LANE)), slots, 1)[0:1, :]
    row = jnp.where(lane < slots, one, jnp.where(lane < 2 * slots, two, -1.0))
    tsend[...] = jnp.broadcast_to(row, tsend.shape)
    trecv[s] = jnp.broadcast_to(row, tsend.shape)

    b0 = basis_ref[0].astype(F32)
    b1 = basis_ref[1].astype(F32)
    zb = jnp.zeros_like(b0)
    bs = [jnp.concatenate([b0, zb], 0).astype(BF16), jnp.concatenate([zb, b1], 0).astype(BF16)]

    cl = jnp.zeros((2 * slots, cols), F32)
    for j in range(2):
        ld_r[j].wait()
        hi, lo = split(rv[j])
        rhi[j] = hi
        cl = cl + (mm(bs[j], hi) + mm(bs[j], lo))
    clv[...] = cl
    clt = jnp.concatenate([cl, jnp.zeros((LANE - 2 * slots, cols), F32)], 0).T
    for q in range(n_sub):
        rsend[q] = clt[q * part:(q + 1) * part, :]
    rrecv[s] = rsend[s]

    extra = jnp.where(wrap_prev, 1, 0) + jnp.where(wrap_next, 1, 0)
    pl.semaphore_wait(barrier, n_sub - 1 + n_grp - 1 + extra)

    sub_at = [{"sub": lax.rem(s + k, n_sub)} for k in range(n_sub)]
    sub_in = [lax.rem(s + n_sub - k, n_sub) for k in range(n_sub)]
    t_copy = [remote(tsend, trecv.at[s], t_sem, k, sub_at[k]) for k in range(1, n_sub)]
    r_copy = [
        remote(rsend.at[lax.rem(s + k, n_sub)], rrecv.at[s], r_sem, k, sub_at[k])
        for k in range(1, n_sub)
    ]
    for c in t_copy:
        c.start()
    for c in r_copy:
        c.start()

    ld_l.wait()
    lone = [split(lv[j]) for j in range(2)]
    for j in range(2):
        lmat[2 * j], lmat[2 * j + 1] = lone[j]
    a_own = mm3(lone[1], lone[0])
    asend[...] = a_own
    a_copy = remote(asend, arecv, a_sem, 0, pair_at)
    a_copy.start()

    btall = jnp.concatenate([b0, b1, jnp.zeros((LANE - 2 * slots, faces), F32)], 0).T
    lane_f = lax.broadcasted_iota(jnp.int32, btall.shape, 1)
    bt0 = jnp.where(lane_f < slots, btall, 0.0)
    bt1 = jnp.where(lane_f < slots, 0.0, btall)
    bt[0] = bt0.astype(BF16)
    bt[1] = bt1.astype(BF16)
    btedge[0] = bt0[0:share]
    btedge[1] = bt1[faces - share:]
    for j in range(2):
        kown[j] = jnp.broadcast_to(coup_ref[j:j + 1, :], (LANE, share)).T

    ld_p.wait()
    d_next = remote(pv.at[1, pl.ds(faces - share, share)], dhalo.at[0], dh_sem, 0, next_at)
    d_prev = remote(pv.at[0, pl.ds(0, share)], dhalo.at[1], dh_sem, 1, prev_at)
    l_next = remote(lp.at[1, pl.ds(faces - share, share)], lhalo.at[0], lh_sem, 0, next_at)
    l_prev = remote(lp.at[0, pl.ds(0, share)], lhalo.at[1], lh_sem, 1, prev_at)
    b_next = remote(btedge.at[1], bhalo.at[0], bh_sem, 0, next_at)
    b_prev = remote(btedge.at[0], bhalo.at[1], bh_sem, 1, prev_at)
    k_prev = remote(kown.at[0], knext, kn_sem, 0, prev_at)
    c_next = remote(cbuf.at[pl.ds(slots, slots)], chalo.at[0], ch_sem, 0, next_at)
    c_prev = remote(cbuf.at[pl.ds(0, slots)], chalo.at[1], ch_sem, 1, prev_at)

    @pl.when(has_next)
    def _():
        b_next.start()
        d_next.start()

    @pl.when(has_prev)
    def _():
        b_prev.start()
        k_prev.start()
        d_prev.start()

    @pl.when(jnp.logical_not(has_prev))
    def _():
        dhalo[0] = jnp.zeros_like(dhalo[0])
        lhalo[0] = jnp.zeros_like(lhalo[0])
        bhalo[0] = jnp.zeros_like(bhalo[0])
        chalo[0] = jnp.zeros_like(chalo[0])

    @pl.when(jnp.logical_not(has_next))
    def _():
        dhalo[1] = jnp.zeros_like(dhalo[1])
        lhalo[1] = jnp.zeros_like(lhalo[1])
        bhalo[1] = jnp.zeros_like(bhalo[1])
        chalo[1] = jnp.zeros_like(chalo[1])
        knext[...] = jnp.zeros_like(knext)

    ld_d.wait()
    for k in range(1, n_sub):
        t_copy[k - 1].wait()
    trow = jnp.concatenate([trecv[q][0:1, :] for q in range(n_sub)], 1)
    rows = lax.broadcasted_iota(jnp.int32, (blk, wide), 0).astype(F32)
    fs = []
    for j in range(2):
        sel = (rows + float(blk * j) == trow).astype(F32).astype(BF16)
        dhi, dlo = split(dv[j])
        fs.append(mm(dhi, sel) + mm(dlo, sel))
    f_pair = [split(fs[0]), split(fs[1])]
    for j in range(2):
        fmat[2 * j], fmat[2 * j + 1] = f_pair[j]
    hb = split(fs[1] - mm3(lone[1], f_pair[0]))

    for k in range(1, n_sub):
        r_copy[k - 1].wait()
    rcat = split(jnp.concatenate([rrecv[q] for q in range(n_sub)], 1))
    b_val = mm3(rcat, hb, NT)
    bv[...] = b_val
    b_copy = remote(bv, brecv, b_sem, 0, pair_at)

    @pl.when(even)
    def _():
        b_copy.start()

    e0v[...] = mm3(rcat, f_pair[0], NT)
    a_copy.wait()
    a_oth = arecv[...]
    a0 = jnp.where(odd, a_oth, a_own)
    a1 = jnp.where(odd, a_own, a_oth)
    a0p, a1p = split(a0), split(a1)
    app = split(mm3(a1p, a0p))
    amat[0], amat[1] = a0p
    amat[2], amat[3] = a1p
    amat[4], amat[5] = app

    def a_of(k):
        return amat[2 * k], amat[2 * k + 1]

    def l_of(k):
        return lmat[2 * k], lmat[2 * k + 1]

    def heavy():
        ld_i.wait()

        def local(c, _):
            at = pl.ds(pl.multiple_of(c * CHUNK, CHUNK), CHUNK)
            for j in range(2):
                lp[j, at, :] = mm(iv[j, at, :], rhi[j])
            return 0

        lax.fori_loop(0, faces // CHUNK, local, 0)

        @pl.when(has_next)
        def _():
            l_next.start()

        @pl.when(has_prev)
        def _():
            l_prev.start()

        ld_s.wait()
        for j in range(2):
            for src, dst in ((pv, ud), (lp, ulp)):
                hi, lo = split(src[j])
                xhi[...] = hi
                xlo[...] = lo

                def apply(c, _, dst=dst, j=j):
                    at = pl.ds(pl.multiple_of(c * CHUNK, CHUNK), CHUNK)
                    block = sv[j, at, :]
                    dst[j, at, :] = mm(block, xhi[...]) + mm(block, xlo[...])
                    return 0

                lax.fori_loop(0, faces // CHUNK, apply, 0)

            hi_lane = j

            def wide_basis(c, _, j=hi_lane):
                at = pl.ds(pl.multiple_of(c * CHUNK, CHUNK), CHUNK)
                w = mm(sv[j, at, :], bt[j])
                whi, wlo = split(w)
                wcat[j, at, 0:LANE] = whi
                wcat[j, at, LANE:2 * LANE] = wlo
                wcat[j, at, 2 * LANE:3 * LANE] = whi
                return 0

            lax.fori_loop(0, faces // CHUNK, wide_basis, 0)

    late = plane >= n_plane // 2

    @pl.when(late)
    def _():
        heavy()

    up = {"grp": 2 * plane + 3}
    up_even = {"grp": 2 * plane + 2}
    down = {"grp": 2 * plane - 2}
    down_odd = {"grp": 2 * plane - 1}
    y_odd = remote(yout, yin, y_sem, 0, up)
    y_even = remote(yout, yin, y_sem, 1, up_even)
    q_copy = remote(qsend, qrecv, q_sem, 0, pair_at)
    t_even = remote(tout, tin, ti_sem, 0, down)
    t_odd = remote(tout, tin, ti_sem, 1, down_odd)

    @pl.when(first_plane)
    def _():
        yin[...] = jnp.zeros_like(yin)

    @pl.when(last_plane)
    def _():
        tin[...] = jnp.zeros_like(tin)

    @pl.when(odd)
    def _():
        b_copy.wait_recv()
        first = brecv[...]
        bpl[...] = bv[...] + mm3(split(first), a_of(1), NT)

        @pl.when(jnp.logical_not(first_plane))
        def _():
            y_odd.wait_recv()

        before = split(yin[...])
        after = bpl[...] + mm3(before, a_of(2), NT)
        yout[...] = after

        @pl.when(jnp.logical_not(last_plane))
        def _():
            y_odd.start()
            y_even.start()

        middle = first + mm3(before, a_of(0), NT)
        y0 = e0v[...] - mm3(split(middle), l_of(0), NT)
        y0v[...] = y0
        y1v[...] = after
        qsend[...] = mm3(split(y0), l_of(0)) - mm3(split(after), a_of(1))
        q_copy.start()

    @pl.when(even)
    def _():
        @pl.when(jnp.logical_not(first_plane))
        def _():
            y_even.wait_recv()

        before = split(yin[...])
        y0 = e0v[...] - mm3(before, l_of(0), NT)
        y1 = bv[...] + mm3(before, a_of(0), NT)
        y0v[...] = y0
        y1v[...] = y1
        bpl[...] = mm3(split(y0), l_of(0)) - mm3(split(y1), a_of(0))

    @pl.when(jnp.logical_not(late))
    def _():
        heavy()

    @pl.when(even)
    def _():
        q_copy.wait_recv()
        q1 = qrecv[...]
        bpl[...] = bpl[...] + mm3(split(q1), a_of(0))

        @pl.when(jnp.logical_not(last_plane))
        def _():
            t_even.wait_recv()

        after = split(tin[...])
        tout[...] = bpl[...] + mm3(after, a_of(2))

        @pl.when(jnp.logical_not(first_plane))
        def _():
            t_even.start()
            t_odd.start()

        y1v[...] = y1v[...] - (q1 + mm3(after, a_of(1)))

    @pl.when(odd)
    def _():
        @pl.when(jnp.logical_not(last_plane))
        def _():
            t_odd.wait_recv()

        y1v[...] = y1v[...] - tin[...]

    w1 = split(y1v[...])
    w0 = split(y0v[...] - mm3(w1, l_of(1)))
    call = mm3(w0, (fmat[0], fmat[1])) + mm3(w1, (fmat[2], fmat[3]))
    for q in range(n_sub):
        csend[q] = call[:, q * LANE:(q + 1) * LANE]
    crecv[s] = csend[s]
    c_copy = [
        remote(csend.at[lax.rem(s + k, n_sub)], crecv.at[s], c_sem, k, sub_at[k])
        for k in range(1, n_sub)
    ]
    for c in c_copy:
        c.start()

    @pl.when(has_prev)
    def _():
        d_next.wait_recv()
        l_next.wait_recv()
        b_next.wait_recv()

    @pl.when(has_next)
    def _():
        d_prev.wait_recv()
        l_prev.wait_recv()
        b_prev.wait_recv()
        k_prev.wait_recv()

    def spread(k):
        return jnp.concatenate([k] * (cols // LANE), 1)

    k0, k1, k2 = spread(kown[0]), spread(kown[1]), spread(knext[...])
    head, tail = pl.ds(0, share), pl.ds(faces - share, share)
    for src, dst, halo in ((pv, ud, dhalo), (lp, ulp, lhalo)):
        dst[0, head, :] = dst[0, head, :] - k0 * halo[0]
        dst[0, tail, :] = dst[0, tail, :] - k1 * src[1, head, :]
        dst[1, head, :] = dst[1, head, :] - k1 * src[0, tail, :]
        dst[1, tail, :] = dst[1, tail, :] - k2 * halo[1]
    for j, at, value in (
        (0, tail, bt[1, head, :]),
        (1, head, bt[0, tail, :]),
    ):
        w = wcat[j, at, 0:LANE].astype(F32) + wcat[j, at, LANE:2 * LANE].astype(F32)
        whi, wlo = split(w - kown[1] * value.astype(F32))
        wcat[j, at, 0:LANE] = whi
        wcat[j, at, LANE:2 * LANE] = wlo
        wcat[j, at, 2 * LANE:3 * LANE] = whi
    edge0 = split(kown[0] * bhalo[0])
    edge1 = split(knext[...] * bhalo[1])
    mx = (mm(bs[0][:, 0:share], edge0[0]) + mm(bs[0][:, 0:share], edge0[1])) + (
        mm(bs[1][:, faces - share:], edge1[0]) + mm(bs[1][:, faces - share:], edge1[1])
    )
    m_own = jnp.zeros((2 * slots, LANE), F32)
    g1 = jnp.zeros((2 * slots, cols), F32)
    g3 = jnp.zeros((2 * slots, cols), F32)
    for j in range(2):
        m_own = m_own + (mm(bs[j], wcat[j, :, 0:LANE]) + mm(bs[j], wcat[j, :, LANE:2 * LANE]))
        hi, lo = split(ulp[j])
        g1 = g1 + (mm(bs[j], hi) + mm(bs[j], lo))
        hi, lo = split(ud[j])
        g3 = g3 + (mm(bs[j], hi) + mm(bs[j], lo))
    acc = [jnp.zeros((8, cols), F32) for _ in range(4)]

    def dots(c, acc):
        at = pl.ds(pl.multiple_of(c * LANE, LANE), LANE)
        acc = list(acc)
        for j in range(2):
            l, p, ul, u, r = lp[j, at, :], pv[j, at, :], ulp[j, at, :], ud[j, at, :], rv[j, at, :]
            for i, x in enumerate((r * l, l * ul, l * u, p * u)):
                acc[i] = acc[i] + jnp.sum(x.reshape(LANE // 8, 8, cols), 0)
        return tuple(acc)

    acc = lax.fori_loop(0, faces // LANE, dots, tuple(acc))
    base = [jnp.sum(x, 0, keepdims=True) for x in acc]

    for c in c_copy:
        c.wait()
    corr = jnp.concatenate([crecv[q] for q in range(n_sub)], 0).T
    cbuf[...] = corr[0:2 * slots]

    @pl.when(has_next)
    def _():
        c_next.start()

    @pl.when(has_prev)
    def _():
        c_prev.start()

    chi, clo = split(corr)
    own = corr[0:2 * slots]
    mhi, mlo = split(m_own)
    mc = mm3((mhi, mlo), (chi, clo))

    @pl.when(has_prev)
    def _():
        c_next.wait_recv()

    @pl.when(has_next)
    def _():
        c_prev.wait_recv()

    cx = jnp.concatenate([chalo[1], chalo[0], jnp.zeros((LANE - 2 * slots, cols), F32)], 0)
    cxp = split(cx)
    mc = mc - mm3(split(mx), cxp)
    rz = base[0] + jnp.sum(clv[...] * own, 0, keepdims=True)
    qa = base[1] + jnp.sum(own * (2.0 * g1 + mc), 0, keepdims=True)
    qb = 2.0 * (base[2] + jnp.sum(own * g3, 0, keepdims=True))
    sums[...] = jnp.concatenate([rz, qa, qb, base[3], jnp.zeros((4, cols), F32)], 0)
    gath1[s] = sums[...]
    s1 = [remote(sums, gath1.at[s], s1_sem, k, sub_at[k]) for k in range(1, n_sub)]
    for c in s1:
        c.start()

    c2 = jnp.concatenate([chi, clo], 0)
    c3 = jnp.concatenate([chi, chi, clo], 0)

    def finish(j):
        def step(c, _):
            at = pl.ds(pl.multiple_of(c * CHUNK, CHUNK), CHUNK)
            block = bt[j, at, :]
            lp[j, at, :] = lp[j, at, :] + mm(jnp.concatenate([block, block], 1), c2)
            ulp[j, at, :] = ulp[j, at, :] + mm(wcat[j, at, :], c3)
            return 0

        lax.fori_loop(0, faces // CHUNK, step, 0)

    if True:
        @pl.when(has_next)
        def _():
            l_next.wait_send()

        @pl.when(has_prev)
        def _():
            l_prev.wait_send()

    for c in s1:
        c.wait()
    total = gath1[0]
    for q in range(1, n_sub):
        total = total + gath1[q]
    mid[...] = total
    gath2[g] = total
    s2 = [
        remote(mid, gath2.at[g], s2_sem, k, {"grp": lax.rem(g + k, n_grp)})
        for k in range(1, n_grp)
    ]
    for c in s2:
        c.start()
    finish(0)
    finish(1)
    ulp[0, head, :] = ulp[0, head, :] - mm3(edge0, cxp)
    ulp[1, tail, :] = ulp[1, tail, :] - mm3(edge1, cxp)
    for c in s2:
        c.wait()
    total = gath2[0]
    for q in range(1, n_grp):
        total = total + gath2[q]
    rz = total[0:1]
    beta = rz / rzp_ref[...]
    step_size = rz / (total[1:2] + beta * (total[2:3] + beta * total[3:4]))

    @pl.when(has_next)
    def _():
        d_next.wait_send()
        b_next.wait_send()
        c_next.wait_send()

    @pl.when(has_prev)
    def _():
        d_prev.wait_send()
        b_prev.wait_send()
        k_prev.wait_send()
        c_prev.wait_send()

    out = []
    for j in range(2):
        for h in range(faces // CHUNK):
            at = pl.ds(h * CHUNK, CHUNK)
            n = j * (faces // CHUNK) + h
            lp[j, at, :] = step_size * (lp[j, at, :] + beta * pv[j, at, :])
            cu = pltpu.make_async_copy(lp.at[j, at], upd_h.at[j, at], out_sem.at[0, n])
            cu.start()
            ulp[j, at, :] = rv[j, at, :] - step_size * (ulp[j, at, :] + beta * ud[j, at, :])
            cn = pltpu.make_async_copy(ulp.at[j, at], new_h.at[j, at], out_sem.at[1, n])
            cn.start()
            out += [cu, cn]

    @pl.when(even)
    def _():
        b_copy.wait_send()

        @pl.when(jnp.logical_not(first_plane))
        def _():
            t_even.wait_send()
            t_odd.wait_send()

    @pl.when(odd)
    def _():
        q_copy.wait_send()

        @pl.when(jnp.logical_not(last_plane))
        def _():
            y_odd.wait_send()
            y_even.wait_send()

    for c in out:
        c.wait()


def shards(
    schur,
    local_inverse,
    coupling,
    basis,
    coarse_map,
    coarse_count,
    diag_inverse,
    chain_factor,
    residual,
    direction,
    rz_prev,
):
    n_sub, n_grp = lax.axis_size("sub"), lax.axis_size("grp")
    subs, faces, cols = residual.shape
    share = coupling.shape[1]
    slots = basis.shape[1]
    blk = diag_inverse.shape[1]
    part = cols // n_sub
    wide = n_sub * LANE
    vm = pltpu.VMEM
    dma = pltpu.SemaphoreType.DMA
    whole = pl.BlockSpec(memory_space=pltpu.VMEM)
    far = pl.BlockSpec(memory_space=pl.ANY)
    strip = vm((part, blk), F32)
    scratch = [
        vm(schur.shape, BF16),
        vm(schur.shape, BF16),
        vm(diag_inverse.shape, F32),
        vm(chain_factor.shape, F32),
        vm(residual.shape, F32),
        vm(residual.shape, F32),
        vm(residual.shape, BF16),
        vm((faces, cols), BF16),
        vm((faces, cols), BF16),
        vm(residual.shape, F32),
        vm(residual.shape, F32),
        vm(residual.shape, F32),
        vm((subs, faces, LANE), BF16),
        vm((subs, faces, 3 * LANE), BF16),
        vm((2, share, LANE), F32),
        vm((2, share, LANE), F32),
        vm((share, LANE), F32),
        vm((8, LANE), jnp.int32),
        vm((8, LANE), F32),
        vm((n_sub, 8, LANE), F32),
        vm((n_sub, part, LANE), F32),
        vm((n_sub, part, LANE), F32),
        vm((blk, blk), F32),
        vm((blk, blk), F32),
        vm((6, blk, blk), BF16),
        vm((4, blk, blk), BF16),
        vm((4, blk, wide), BF16),
        strip,
        strip,
        strip,
        strip,
        strip,
        strip,
        strip,
        strip,
        strip,
        strip,
        strip,
        strip,
        vm((n_sub, part, LANE), F32),
        vm((n_sub, part, LANE), F32),
        vm((2 * slots, cols), F32),
        vm((2, slots, cols), F32),
        vm((2, share, cols), F32),
        vm((2, share, cols), F32),
        vm((2, share, LANE), F32),
        vm((2 * slots, cols), F32),
        vm((8, LANE), F32),
        vm((8, LANE), F32),
        vm((8, cols), F32),
        vm((n_sub, 8, cols), F32),
        vm((8, cols), F32),
        vm((n_grp, 8, cols), F32),
        dma((7,)),
        dma((2, 2 * (faces // CHUNK))),
        dma((2, n_sub)),
        dma((2, n_sub)),
        dma((2, 1)),
        dma((2, 1)),
        dma((2, 2)),
        dma((2, 1)),
        dma((2, 2)),
        dma((2, n_sub)),
        dma((2, 2)),
        dma((2, 2)),
        dma((2, 2)),
        dma((2, 2)),
        dma((2, 1)),
        dma((2, n_sub)),
        dma((2, n_grp)),
    ]
    return pl.pallas_call(
        functools.partial(kernel, n_sub, n_grp),
        out_shape=(
            jax.ShapeDtypeStruct(residual.shape, F32),
            jax.ShapeDtypeStruct(residual.shape, F32),
        ),
        in_specs=[pl.BlockSpec(memory_space=pltpu.SMEM)] + [whole] * 4 + [far] * 6,
        out_specs=(far, far),
        scratch_shapes=scratch,
        compiler_params=pltpu.CompilerParams(
            collective_id=0, has_side_effects=True, vmem_limit_bytes=60 * 2**20
        ),
    )(
        coarse_count,
        coupling,
        basis,
        coarse_map,
        rz_prev[None, :],
        schur,
        local_inverse,
        diag_inverse,
        chain_factor,
        residual,
        direction,
    )


def solution(mesh):
    return jax.shard_map(
        shards,
        mesh=mesh,
        in_specs=(
            P(("sub", "grp"), None, None),
            P(("sub", "grp"), None, None),
            P(("sub", "grp"), None),
            P(("sub", "grp"), None, None),
            P(("sub", "grp"), None),
            P(("sub", "grp")),
            P("grp", None, None),
            P("grp", None, None),
            P(("sub", "grp"), None, None),
            P(("sub", "grp"), None, None),
            P(),
        ),
        out_specs=(P(("sub", "grp"), None, None), P(("sub", "grp"), None, None)),
        check_vma=False,
    )
```

time: 379 us -> 102 us (0.27)
  waiting for transfers between devices: 155 us -> 0 us
  Pallas kernels: 0 us -> 94.8 us
  blocking collectives: 94.3 us -> 0 us
  matrix products: 55.7 us -> 0 us
  starting transfers between devices: 55 us -> 0 us
  other arithmetic: 11.9 us -> 0 us
    ppermute x18 -> x0, waiting for transfers between devices: 155 us -> none  [shifted(): lax.ppermute(value, axis, [(source, source + steps) for source in range(l...]
    pallas_call x0 -> x1, Pallas kernels: none -> 94.8 us  [shards(): pl.pallas_call(functools.partial(kernel, n_sub, n_grp), out_shape=(jax.Sh...]
    psum x2 -> x0, blocking collectives: 82.1 us -> none  [the longest x1 41.1 us: shards(): lax.psum(jnp.sum(residual * precond, axis=(0, 1)), ('sub', 'grp'))]
    dot_general x62 -> x0, matrix products: 55.7 us -> none  [the longest x58 35.4 us: product(): jnp.dot(left_side, right_side, precision=lax.Precision.HIGHEST, preferred...]
    ppermute x18 -> x0, starting transfers between devices: 55 us -> none  [shifted(): lax.ppermute(value, axis, [(source, source + steps) for source in range(l...]
    sub x1 -> x0, other arithmetic: 6.97 us -> none  [shards(): return (step_size * new_dir, residual - step_size * applied)]
    unnamed x1 -> x0, blocking collectives: 6.38 us -> none
    all_gather x1 -> x0, blocking collectives: 5.88 us -> none  [shards(): lax.all_gather(coarse_local, 'sub', axis=0, tiled=True)]
  transfers between devices with their start and end apart: 18 -> 0, of which waited for: 18 -> 0; matrix products, arithmetic and copies ran while one was open for 2% -> 0% of each run, Pallas kernels for 0% -> 0%
where the time goes in v1:
time: 102 us
  Pallas kernels  94.8 us (93%)
  local copies, waits for them, and re-layouts  6.82 us (7%)
    pallas_call x1, Pallas kernels, shards(): pl.pallas_call(functools.partial(kernel, n_sub, n_grp), out_shape=(jax.Sh...  94.8 us
    unnamed x4, local copies, waits for them, and re-layouts  5.58 us

profile of v1, /device:TPU:0, one launch (start us, length us, event | category | flops | bytes accessed | tf_op | source)
XLA Modules:
  0.0 102.2 jit_solution(15260173161281107123)
XLA Ops:
  0.6 1.2 %broadcast_in_dim.3.rzp_ref = f32[1,384]{1,0:T(1,128)} reshape(f32[384]{0:T(512)} %param.21) | data formatting | bytes 3072 | tf_op jit(solution)/shard_map/broadcast_in_dim | solution.py:795
  1.9 94.8 %shard_map.122 = (f32[2,1024,384]{2,1,0:T(8,128)}, f32[2,1024,384]{2,1,0:T(8,128)}) custom-call(s32[2]{0:T(128)} %count_ref.1, f32[2,256]{1,0:T(2,128)} %coup_ref.1, bf16[2,24,1024]{2,1,0:T(8,128)(2,1)} %basis_ref.1, s32[2,24]{1,0:T(2,128)} %cmap_ref.1, f32[1,384]{1,0:T(1,128)} %broadcast_in_dim.3.rzp_ref, bf16[2,1024,1024]{2,1,0:T(8,128)(2,1)} %schur_h.1, ...), custom_call_target="tpu_custom_call" | custom-call | tf_op jit(solution)/shard_map/pallas_call | solution.py:778
  96.7 0.0 copy-start
  96.7 3.9 %copy.15 = f32[2,1024,384]{2,1,0:T(8,128)} copy(f32[2,1024,384]{2,1,0:T(8,128)} %get-tuple-element.4) | data formatting | bytes 6291456
  100.6 0.0 copy-done
  100.6 1.7 %copy.16 = f32[2,1024,384]{2,1,0:T(8,128)} copy(f32[2,1024,384]{2,1,0:T(8,128)S(1)} %copy-done) | data formatting | bytes 6291456
Async XLA Ops:
  96.7 3.9 %copy-start = (f32[2,1024,384]{2,1,0:T(8,128)S(1)}, f32[2,1024,384]{2,1,0:T(8,128)}, u32[]{:S(2)}) copy-start(f32[2,1024,384]{2,1,0:T(8,128)} %get-tuple-element.5) | copy-start | bytes 9437188

commit v2 on v1

--- a/solution.py
+++ b/solution.py
@@ -35,15 +35,16 @@
     coup_ref,
     basis_ref,
     cmap_ref,
-    rzp_ref,
     schur_h,
     linv_h,
     diag_h,
     chain_h,
     res_h,
     dir_h,
-    upd_h,
-    new_h,
+    p_h,
+    up_h,
+    ud_h,
+    sums_out,
     sv,
     iv,
     dv,
@@ -58,9 +59,8 @@
     ud,
     bt,
     wcat,
-    btedge,
+    bsend,
     kown,
-    knext,
     mapv,
     tsend,
     trecv,
@@ -91,8 +91,6 @@
     lhalo,
     bhalo,
     clv,
-    gmat,
-    mmat,
     sums,
     gath1,
     mid,
@@ -111,7 +109,6 @@
     dh_sem,
     lh_sem,
     bh_sem,
-    kn_sem,
     s1_sem,
     s2_sem,
 ):
@@ -187,6 +184,25 @@
             barrier, inc=1, device_id=next_at, device_id_type=pl.DeviceIdType.MESH
         )
 
+    b0 = basis_ref[0].astype(F32)
+    b1 = basis_ref[1].astype(F32)
+    zb = jnp.zeros_like(b0)
+    bs = [jnp.concatenate([b0, zb], 0).astype(BF16), jnp.concatenate([zb, b1], 0).astype(BF16)]
+    crow = jnp.broadcast_to(coup_ref[0:1, :], (8, share))
+    bsend[0] = jnp.concatenate([b0[:, 0:share], crow], 0)
+    bsend[1] = jnp.concatenate([b1[:, faces - share:], crow], 0)
+
+    d_next = remote(dir_h.at[1, pl.ds(faces - share, share)], dhalo.at[0], dh_sem, 0, next_at)
+    d_prev = remote(dir_h.at[0, pl.ds(0, share)], dhalo.at[1], dh_sem, 1, prev_at)
+    l_next = remote(lp.at[1, pl.ds(faces - share, share)], lhalo.at[0], lh_sem, 0, next_at)
+    l_prev = remote(lp.at[0, pl.ds(0, share)], lhalo.at[1], lh_sem, 1, prev_at)
+    b_next = remote(bsend.at[1], bhalo.at[0], bh_sem, 0, next_at)
+    b_prev = remote(bsend.at[0], bhalo.at[1], bh_sem, 1, prev_at)
+    c_next = remote(cbuf.at[pl.ds(slots, slots)], chalo.at[0], ch_sem, 0, next_at)
+    c_prev = remote(cbuf.at[pl.ds(0, slots)], chalo.at[1], ch_sem, 1, prev_at)
+    extra = jnp.where(wrap_prev, 1, 0) + jnp.where(wrap_next, 1, 0)
+    pl.semaphore_wait(barrier, n_sub - 1 + n_grp - 1 + extra)
+
     mapv[...] = jnp.zeros_like(mapv)
     mapv[0:2, 0:slots] = cmap_ref[...]
     lane = lax.broadcasted_iota(jnp.int32, (1, LANE), 1)
@@ -196,11 +212,6 @@
     row = jnp.where(lane < slots, one, jnp.where(lane < 2 * slots, two, -1.0))
     tsend[...] = jnp.broadcast_to(row, tsend.shape)
     trecv[s] = jnp.broadcast_to(row, tsend.shape)
-
-    b0 = basis_ref[0].astype(F32)
-    b1 = basis_ref[1].astype(F32)
-    zb = jnp.zeros_like(b0)
-    bs = [jnp.concatenate([b0, zb], 0).astype(BF16), jnp.concatenate([zb, b1], 0).astype(BF16)]
 
     cl = jnp.zeros((2 * slots, cols), F32)
     for j in range(2):
@@ -214,9 +225,6 @@
         rsend[q] = clt[q * part:(q + 1) * part, :]
     rrecv[s] = rsend[s]
 
-    extra = jnp.where(wrap_prev, 1, 0) + jnp.where(wrap_next, 1, 0)
-    pl.semaphore_wait(barrier, n_sub - 1 + n_grp - 1 + extra)
-
     sub_at = [{"sub": lax.rem(s + k, n_sub)} for k in range(n_sub)]
     sub_in = [lax.rem(s + n_sub - k, n_sub) for k in range(n_sub)]
     t_copy = [remote(tsend, trecv.at[s], t_sem, k, sub_at[k]) for k in range(1, n_sub)]
@@ -238,38 +246,39 @@
     a_copy = remote(asend, arecv, a_sem, 0, pair_at)
     a_copy.start()
 
+    @pl.when(has_next)
+    def _():
+        b_next.start()
+
+    @pl.when(has_prev)
+    def _():
+        b_prev.start()
+
+    def send_direction():
+        @pl.when(has_next)
+        def _():
+            d_next.start()
+
+        @pl.when(has_prev)
+        def _():
+            d_prev.start()
+
+    late = plane >= n_plane // 2
+
+    @pl.when(late)
+    def _():
+        send_direction()
+
     btall = jnp.concatenate([b0, b1, jnp.zeros((LANE - 2 * slots, faces), F32)], 0).T
     lane_f = lax.broadcasted_iota(jnp.int32, btall.shape, 1)
     bt0 = jnp.where(lane_f < slots, btall, 0.0)
     bt1 = jnp.where(lane_f < slots, 0.0, btall)
     bt[0] = bt0.astype(BF16)
     bt[1] = bt1.astype(BF16)
-    btedge[0] = bt0[0:share]
-    btedge[1] = bt1[faces - share:]
     for j in range(2):
         kown[j] = jnp.broadcast_to(coup_ref[j:j + 1, :], (LANE, share)).T
 
     ld_p.wait()
-    d_next = remote(pv.at[1, pl.ds(faces - share, share)], dhalo.at[0], dh_sem, 0, next_at)
-    d_prev = remote(pv.at[0, pl.ds(0, share)], dhalo.at[1], dh_sem, 1, prev_at)
-    l_next = remote(lp.at[1, pl.ds(faces - share, share)], lhalo.at[0], lh_sem, 0, next_at)
-    l_prev = remote(lp.at[0, pl.ds(0, share)], lhalo.at[1], lh_sem, 1, prev_at)
-    b_next = remote(btedge.at[1], bhalo.at[0], bh_sem, 0, next_at)
-    b_prev = remote(btedge.at[0], bhalo.at[1], bh_sem, 1, prev_at)
-    k_prev = remote(kown.at[0], knext, kn_sem, 0, prev_at)
-    c_next = remote(cbuf.at[pl.ds(slots, slots)], chalo.at[0], ch_sem, 0, next_at)
-    c_prev = remote(cbuf.at[pl.ds(0, slots)], chalo.at[1], ch_sem, 1, prev_at)
-
-    @pl.when(has_next)
-    def _():
-        b_next.start()
-        d_next.start()
-
-    @pl.when(has_prev)
-    def _():
-        b_prev.start()
-        k_prev.start()
-        d_prev.start()
 
     @pl.when(jnp.logical_not(has_prev))
     def _():
@@ -284,7 +293,6 @@
         lhalo[1] = jnp.zeros_like(lhalo[1])
         bhalo[1] = jnp.zeros_like(bhalo[1])
         chalo[1] = jnp.zeros_like(chalo[1])
-        knext[...] = jnp.zeros_like(knext)
 
     ld_d.wait()
     for k in range(1, n_sub):
@@ -312,6 +320,10 @@
     def _():
         b_copy.start()
 
+        @pl.when(jnp.logical_not(late))
+        def _():
+            send_direction()
+
     e0v[...] = mm3(rcat, f_pair[0], NT)
     a_copy.wait()
     a_oth = arecv[...]
@@ -329,25 +341,32 @@
     def l_of(k):
         return lmat[2 * k], lmat[2 * k + 1]
 
+    ld_i.wait()
+
+    def local(c, _):
+        at = pl.ds(pl.multiple_of(c * CHUNK, CHUNK), CHUNK)
+        for j in range(2):
+            lp[j, at, :] = mm(iv[j, at, :], rhi[j])
+        return 0
+
+    lax.fori_loop(0, faces // CHUNK, local, 0)
+
+    def send_local():
+        @pl.when(has_next)
+        def _():
+            l_next.start()
+
+        @pl.when(has_prev)
+        def _():
+            l_prev.start()
+
+    @pl.when(jnp.logical_or(even, last_plane))
+    def _():
+        send_local()
+
+    half = faces // 2
+
     def heavy():
-        ld_i.wait()
-
-        def local(c, _):
-            at = pl.ds(pl.multiple_of(c * CHUNK, CHUNK), CHUNK)
-            for j in range(2):
-                lp[j, at, :] = mm(iv[j, at, :], rhi[j])
-            return 0
-
-        lax.fori_loop(0, faces // CHUNK, local, 0)
-
-        @pl.when(has_next)
-        def _():
-            l_next.start()
-
-        @pl.when(has_prev)
-        def _():
-            l_prev.start()
-
         ld_s.wait()
         for j in range(2):
             for src, dst in ((pv, ud), (lp, ulp)):
@@ -356,12 +375,12 @@
                 xlo[...] = lo
 
                 def apply(c, _, dst=dst, j=j):
-                    at = pl.ds(pl.multiple_of(c * CHUNK, CHUNK), CHUNK)
+                    at = pl.ds(pl.multiple_of(c * half, half), half)
                     block = sv[j, at, :]
                     dst[j, at, :] = mm(block, xhi[...]) + mm(block, xlo[...])
                     return 0
 
-                lax.fori_loop(0, faces // CHUNK, apply, 0)
+                lax.fori_loop(0, faces // half, apply, 0)
 
             hi_lane = j
 
@@ -375,8 +394,6 @@
                 return 0
 
             lax.fori_loop(0, faces // CHUNK, wide_basis, 0)
-
-    late = plane >= n_plane // 2
 
     @pl.when(late)
     def _():
@@ -425,6 +442,14 @@
         y1v[...] = after
         qsend[...] = mm3(split(y0), l_of(0)) - mm3(split(after), a_of(1))
         q_copy.start()
+
+        @pl.when(jnp.logical_not(late))
+        def _():
+            send_direction()
+
+        @pl.when(jnp.logical_not(last_plane))
+        def _():
+            send_local()
 
     @pl.when(even)
     def _():
@@ -484,6 +509,19 @@
     for c in c_copy:
         c.start()
 
+    for c in c_copy:
+        c.wait()
+    corr = jnp.concatenate([crecv[q] for q in range(n_sub)], 0).T
+    cbuf[...] = corr[0:2 * slots]
+
+    @pl.when(has_next)
+    def _():
+        c_next.start()
+
+    @pl.when(has_prev)
+    def _():
+        c_prev.start()
+
     @pl.when(has_prev)
     def _():
         d_next.wait_recv()
@@ -495,12 +533,16 @@
         d_prev.wait_recv()
         l_prev.wait_recv()
         b_prev.wait_recv()
-        k_prev.wait_recv()
 
     def spread(k):
         return jnp.concatenate([k] * (cols // LANE), 1)
 
-    k0, k1, k2 = spread(kown[0]), spread(kown[1]), spread(knext[...])
+    gap = jnp.zeros((slots, share), F32)
+    rest = jnp.zeros((LANE - 2 * slots, share), F32)
+    bprev = jnp.concatenate([gap, bhalo[0][0:slots], rest], 0).T
+    bnext = jnp.concatenate([bhalo[1][0:slots], gap, rest], 0).T
+    knext = jnp.broadcast_to(bhalo[1][slots:slots + 1], (LANE, share)).T
+    k0, k1, k2 = spread(kown[0]), spread(kown[1]), spread(knext)
     head, tail = pl.ds(0, share), pl.ds(faces - share, share)
     for src, dst, halo in ((pv, ud, dhalo), (lp, ulp, lhalo)):
         dst[0, head, :] = dst[0, head, :] - k0 * halo[0]
@@ -516,8 +558,8 @@
         wcat[j, at, 0:LANE] = whi
         wcat[j, at, LANE:2 * LANE] = wlo
         wcat[j, at, 2 * LANE:3 * LANE] = whi
-    edge0 = split(kown[0] * bhalo[0])
-    edge1 = split(knext[...] * bhalo[1])
+    edge0 = split(kown[0] * bprev)
+    edge1 = split(knext * bnext)
     mx = (mm(bs[0][:, 0:share], edge0[0]) + mm(bs[0][:, 0:share], edge0[1])) + (
         mm(bs[1][:, faces - share:], edge1[0]) + mm(bs[1][:, faces - share:], edge1[1])
     )
@@ -530,6 +572,8 @@
         g1 = g1 + (mm(bs[j], hi) + mm(bs[j], lo))
         hi, lo = split(ud[j])
         g3 = g3 + (mm(bs[j], hi) + mm(bs[j], lo))
+    out_d = pltpu.make_async_copy(ud, ud_h, out_sem.at[4])
+    out_d.start()
     acc = [jnp.zeros((8, cols), F32) for _ in range(4)]
 
     def dots(c, acc):
@@ -543,19 +587,6 @@
 
     acc = lax.fori_loop(0, faces // LANE, dots, tuple(acc))
     base = [jnp.sum(x, 0, keepdims=True) for x in acc]
-
-    for c in c_copy:
-        c.wait()
-    corr = jnp.concatenate([crecv[q] for q in range(n_sub)], 0).T
-    cbuf[...] = corr[0:2 * slots]
-
-    @pl.when(has_next)
-    def _():
-        c_next.start()
-
-    @pl.when(has_prev)
-    def _():
-        c_prev.start()
 
     chi, clo = split(corr)
     own = corr[0:2 * slots]
@@ -617,18 +648,23 @@
     ]
     for c in s2:
         c.start()
-    finish(0)
-    finish(1)
-    ulp[0, head, :] = ulp[0, head, :] - mm3(edge0, cxp)
-    ulp[1, tail, :] = ulp[1, tail, :] - mm3(edge1, cxp)
+    out = []
+    for j in range(2):
+        finish(j)
+        if j == 0:
+            ulp[0, head, :] = ulp[0, head, :] - mm3(edge0, cxp)
+        else:
+            ulp[1, tail, :] = ulp[1, tail, :] - mm3(edge1, cxp)
+        out.append(pltpu.make_async_copy(lp.at[j], p_h.at[j], out_sem.at[2 * j]))
+        out.append(pltpu.make_async_copy(ulp.at[j], up_h.at[j], out_sem.at[2 * j + 1]))
+        out[-2].start()
+        out[-1].start()
     for c in s2:
         c.wait()
     total = gath2[0]
     for q in range(1, n_grp):
         total = total + gath2[q]
-    rz = total[0:1]
-    beta = rz / rzp_ref[...]
-    step_size = rz / (total[1:2] + beta * (total[2:3] + beta * total[3:4]))
+    sums_out[...] = total
 
     @pl.when(has_next)
     def _():
@@ -640,21 +676,7 @@
     def _():
         d_prev.wait_send()
         b_prev.wait_send()
-        k_prev.wait_send()
         c_prev.wait_send()
-
-    out = []
-    for j in range(2):
-        for h in range(faces // CHUNK):
-            at = pl.ds(h * CHUNK, CHUNK)
-            n = j * (faces // CHUNK) + h
-            lp[j, at, :] = step_size * (lp[j, at, :] + beta * pv[j, at, :])
-            cu = pltpu.make_async_copy(lp.at[j, at], upd_h.at[j, at], out_sem.at[0, n])
-            cu.start()
-            ulp[j, at, :] = rv[j, at, :] - step_size * (ulp[j, at, :] + beta * ud[j, at, :])
-            cn = pltpu.make_async_copy(ulp.at[j, at], new_h.at[j, at], out_sem.at[1, n])
-            cn.start()
-            out += [cu, cn]
 
     @pl.when(even)
     def _():
@@ -674,6 +696,7 @@
             y_odd.wait_send()
             y_even.wait_send()
 
+    out_d.wait()
     for c in out:
         c.wait()
 
@@ -718,9 +741,8 @@
         vm(residual.shape, F32),
         vm((subs, faces, LANE), BF16),
         vm((subs, faces, 3 * LANE), BF16),
+        vm((2, slots + 8, share), F32),
         vm((2, share, LANE), F32),
-        vm((2, share, LANE), F32),
-        vm((share, LANE), F32),
         vm((8, LANE), jnp.int32),
         vm((8, LANE), F32),
         vm((n_sub, 8, LANE), F32),
@@ -749,16 +771,14 @@
         vm((2, slots, cols), F32),
         vm((2, share, cols), F32),
         vm((2, share, cols), F32),
-        vm((2, share, LANE), F32),
+        vm((2, slots + 8, share), F32),
         vm((2 * slots, cols), F32),
-        vm((8, LANE), F32),
-        vm((8, LANE), F32),
         vm((8, cols), F32),
         vm((n_sub, 8, cols), F32),
         vm((8, cols), F32),
         vm((n_grp, 8, cols), F32),
         dma((7,)),
-        dma((2, 2 * (faces // CHUNK))),
+        dma((5,)),
         dma((2, n_sub)),
         dma((2, n_sub)),
         dma((2, 1)),
@@ -771,18 +791,15 @@
         dma((2, 2)),
         dma((2, 2)),
         dma((2, 2)),
-        dma((2, 1)),
         dma((2, n_sub)),
         dma((2, n_grp)),
     ]
-    return pl.pallas_call(
+    big = jax.ShapeDtypeStruct(residual.shape, F32)
+    precond, applied_p, applied_d, dots = pl.pallas_call(
         functools.partial(kernel, n_sub, n_grp),
-        out_shape=(
-            jax.ShapeDtypeStruct(residual.shape, F32),
-            jax.ShapeDtypeStruct(residual.shape, F32),
-        ),
-        in_specs=[pl.BlockSpec(memory_space=pltpu.SMEM)] + [whole] * 4 + [far] * 6,
-        out_specs=(far, far),
+        out_shape=(big, big, big, jax.ShapeDtypeStruct((8, cols), F32)),
+        in_specs=[pl.BlockSpec(memory_space=pltpu.SMEM)] + [whole] * 3 + [far] * 6,
+        out_specs=(far, far, far, whole),
         scratch_shapes=scratch,
         compiler_params=pltpu.CompilerParams(
             collective_id=0, has_side_effects=True, vmem_limit_bytes=60 * 2**20
@@ -792,13 +809,18 @@
         coupling,
         basis,
         coarse_map,
-        rz_prev[None, :],
         schur,
         local_inverse,
         diag_inverse,
         chain_factor,
         residual,
         direction,
+    )
+    beta = dots[0] / rz_prev
+    step = dots[0] / (dots[1] + beta * (dots[2] + beta * dots[3]))
+    return (
+        step * (precond + beta * direction),
+        residual - step * (applied_p + beta * applied_d),
     )
 
 

time: 102 us -> 101 us (level)
  other arithmetic: 0 us -> 8.11 us
  local copies, waits for them, and re-layouts: 6.82 us -> 0.89 us
  Pallas kernels: 94.8 us -> 91.1 us
    sub x0 -> x1, other arithmetic: none -> 8.09 us  [shards(): residual - step * (applied_p + beta * applied_d)]
    unnamed x4, local copies, waits for them, and re-layouts: 5.58 us -> 0.01 us
    pallas_call x1, Pallas kernels: 94.8 us -> 91.1 us  [shards(): pl.pallas_call(functools.partial(kernel, n_sub, n_grp), out_shape=(big, b...]
    broadcast_in_dim x1 -> x0, local copies, waits for them, and re-layouts: 1.25 us -> none  [shards(): rz_prev[None, :]]
where the time goes in v2:
time: 101 us
  Pallas kernels  91.1 us (90%)
  other arithmetic  8.11 us (8%)
    pallas_call x1, Pallas kernels, shards(): pl.pallas_call(functools.partial(kernel, n_sub, n_grp), out_shape=(big, b...  91.1 us
    sub x1, other arithmetic, shards(): residual - step * (applied_p + beta * applied_d)  8.09 us

profile of v2, /device:TPU:0, one launch (start us, length us, event | category | flops | bytes accessed | tf_op | source)
XLA Modules:
  0.0 100.7 jit_solution(16683369539853291989)
XLA Ops:
  0.6 0.0 copy-start
  0.6 0.0 copy-start.1
  0.7 91.1 %shard_map.122 = (f32[2,1024,384]{2,1,0:T(8,128)}, f32[2,1024,384]{2,1,0:T(8,128)}, f32[2,1024,384]{2,1,0:T(8,128)}, f32[8,384]{1,0:T(8,128)}) custom-call(s32[2]{0:T(128)} %count_ref.1, f32[2,256]{1,0:T(2,128)} %coup_ref.1, bf16[2,24,1024]{2,1,0:T(8,128)(2,1)} %basis_ref.1, s32[2,24]{1,0:T(2,128)} %cmap_ref.1, bf16[2,1024,1024]{2,1,0:T(8,128)(2,1)} %schur_h.1, ...), custom_call_target="tpu_custom_call" | custom-call | tf_op jit(solution)/shard_map/pallas_call | solution.py:798
  91.7 0.9 slice_reduce_fusion
  92.6 0.0 copy-done.1
  92.6 0.0 copy-done
  92.6 8.1 %multiply_subtract_fusion = (f32[2,1024,384]{2,1,0:T(8,128)}, f32[2,1024,384]{2,1,0:T(8,128)}) fusion(f32[2,1024,384]{2,1,0:T(8,128)S(1)} %copy-done, f32[2,1024,384]{2,1,0:T(8,128)} %get-tuple-element.8, f32[2,1024,384]{2,1,0:T(8,128)} %get-tuple-element.9, f32[384]{0:T(512)S(1)} %get-tuple-element.15, f32[384]{0:T(512)S(1)} %get-tuple-element.14, ...), kind=kLoop, calls=%fused_computation | loop fusion | flops 5505024 | bytes 22023168 | tf_op jit(solution)/shard_map/sub | solution.py:823
  (1 shorter events, 0.0 us)
Async XLA Ops:
  0.6 92.0 %copy-start = (f32[2,1024,384]{2,1,0:T(8,128)S(1)}, f32[2,1024,384]{2,1,0:T(8,128)}, u32[]{:S(2)}) copy-start(f32[2,1024,384]{2,1,0:T(8,128)} %res_h.1) | copy-start | bytes 9437188
  0.6 92.0 %copy-start.1 = (f32[384]{0:T(512)S(1)}, f32[384]{0:T(512)}, u32[]{:S(2)}) copy-start(f32[384]{0:T(512)} %param.21) | copy-start | bytes 4612
